TPU v7x, 256 devices: a whole 4x4x8 slice. The times are simulated.
256 devices in a mesh: leaf: 128 (over y, x, z), sub: 2 (over core).
Axes of the slice: x: 4, y: 4, z: 8, core: 2. Of those that a mesh axis runs over, the one named last changes fastest.
Arguments:
- rhs: float32 [64, 524288], P(None, ('leaf', 'sub')), may hold values from -6 to 6
- points: float32 [3, 524288], P(None, ('leaf', 'sub')), may hold values from 0 to 1, as said below
- basis: float32 [64, 524288], P(None, ('leaf', 'sub')), may hold values from -0.125 to 0.125
- decay: float32 [64], replicated, may hold values from 0.4 to 0.98
- near_list: int32 [2048, 8], P(('leaf', 'sub')), may hold values from 0 to 2047, as said below
- near_count: int32 [2048], P(('leaf', 'sub')), may hold values from 1 to 8, as said below
Outputs:
- solution: float32 [64, 524288], P(None, ('leaf', 'sub'))
- residual: float32 [64, 524288], P(None, ('leaf', 'sub'))
Inputs may be any that keep to these rules, and one draw needn't show every extreme that they name: The points of leaf g lie in the g-th cell of the Morton order of a regular subdivision of the unit cube: bit b of g is bit b // 3 of the cell's index along dimension b % 3. `near_list`: in column k of the list, all leaves of device d name distinct leaves of one device d + s, with s in -1, 0, +1 the same for the whole column and wrapping around the ends of the device order; every leaf is named exactly once in each column. `near_count`: leaf 0 uses all 8 slots.
All inputs are finite; a program needn't handle non-finite values.
Results may differ from a plain program's by a relative error of at most 0.0055.
Values may be sent and summed in bfloat16 or wider, within the bound.
A program may use at most 128 MiB of HBM per device.

v0:
```python
import jax
import jax.numpy as jnp
from jax import lax
from jax.sharding import PartitionSpec as P

LEAF = 256
NEAR = 8
ITERS = 3


def shifted(shard, axis, by):
    peers = lax.axis_size(axis)
    return lax.ppermute(shard, axis, [(i, (i + by) % peers) for i in range(peers)])


def partner_2(value, axis, stride):
    mask = 2**stride
    pairs = [(source, source ^ mask) for source in range(lax.axis_size(axis))]
    return lax.ppermute(value, axis, pairs)


def kernel(first, second):
    diff = first[..., :, :, None] - second[..., :, None, :]
    dist2 = jnp.sum(diff * diff, axis=-3)
    scaled = jnp.sqrt(3.0 * (dist2 + 0.0001)) / 0.08
    return (1.0 + scaled) * jnp.exp(-scaled)


def side_points(value, offset):
    return shifted(value, ("leaf", "sub"), offset)


def side_values(value, offset):
    return shifted(value, ("leaf", "sub"), offset)


def send_back(value, offset):
    return shifted(value.astype(jnp.bfloat16), ("leaf", "sub"), offset).astype(value.dtype)


def side_mult(value, offset):
    return shifted(value, ("leaf", "sub"), offset)


def column_norms(field):
    return lax.psum(jnp.sum(field * field, axis=1), ("leaf", "sub"))


def level_weight(decay, level):
    return jnp.power(decay, level) * jnp.power(0.5, (level - 1.0) / 2.0)


def body(rhs, points, basis, decay, near_list, near_count):
    nrows, npts = rhs.shape
    nleaves = npts // LEAF
    ndev = lax.axis_size("leaf") * lax.axis_size("sub")
    total_leaves = nleaves * ndev
    my_index = lax.axis_index(("leaf", "sub"))
    hp = lax.Precision.HIGHEST
    coords = points.reshape(3, nleaves, LEAF).transpose(1, 0, 2)
    coord_pool = jnp.concatenate([side_points(coords, 1), coords, side_points(coords, -1)], axis=0)
    pool_ids = jnp.arange(3 * nleaves, dtype=jnp.int32)
    slot_ids = jnp.arange(NEAR, dtype=jnp.int32)
    local_slot = (near_list - (my_index - 1) * nleaves) % total_leaves
    active = (slot_ids[None, :] < near_count[:, None]).astype(jnp.float32)
    onehot = (local_slot[:, :, None] == pool_ids[None, None, :]).astype(jnp.float32) * active[
        :, :, None
    ]
    self_weight = jnp.sum(active, axis=1)
    pool_mult = jnp.sum(onehot, axis=(0, 1))
    self_weight = (
        self_weight
        + pool_mult[nleaves : 2 * nleaves]
        + side_mult(pool_mult[:nleaves], -1)
        + side_mult(pool_mult[2 * nleaves :], 1)
    )
    solution = jnp.zeros_like(rhs)
    residual = rhs
    direction = rhs
    norm_now = column_norms(residual)
    for step in range(ITERS):
        rounded = direction.astype(jnp.bfloat16).reshape(nrows, nleaves, LEAF).transpose(1, 0, 2)
        pool = jnp.concatenate([side_values(rounded, 1), rounded, side_values(rounded, -1)], axis=0)

        def leaf_work(args):
            leaf_pts, leaf_vals, leaf_slots, weights, own_weight = args
            part_pts = coord_pool[leaf_slots]
            part_vals = pool[leaf_slots]
            tiles = kernel(leaf_pts[None], part_pts).astype(jnp.bfloat16) * weights[
                :, None, None
            ].astype(jnp.bfloat16)
            own_tile = kernel(leaf_pts, leaf_pts).astype(jnp.bfloat16)
            forward = jnp.einsum(
                "kcb,kab->ca", part_vals, tiles, preferred_element_type=jnp.float32
            )
            forward = forward + own_weight * jnp.einsum(
                "cb,ab->ca", leaf_vals, own_tile, preferred_element_type=jnp.float32
            )
            backward = jnp.einsum(
                "ca,kab->kcb", leaf_vals, tiles, preferred_element_type=jnp.float32
            )
            return (forward, backward)

        forward, backward = lax.map(leaf_work, (coords, rounded, local_slot, active, self_weight))
        pool_back = jnp.einsum("ikp,ikcl->pcl", onehot, backward, precision=hp)
        near = forward + pool_back[nleaves : 2 * nleaves]
        near = near + send_back(pool_back[:nleaves], -1) + send_back(pool_back[2 * nleaves :], 1)
        near = near.transpose(1, 0, 2).reshape(nrows, npts)
        coeffs = jnp.dot(basis, direction.T, precision=hp)
        sibling = partner_2(coeffs, "sub", 0)
        mixed = coeffs + level_weight(decay, 1.0)[:, None] * sibling
        pair_sum = coeffs + sibling
        gathered_sum = pair_sum
        for bit in range(lax.axis_size("leaf").bit_length() - 1):
            partner = partner_2(gathered_sum, "leaf", bit)
            mixed = mixed + level_weight(decay, float(bit + 2))[:, None] * partner
            gathered_sum = gathered_sum + partner
        far = jnp.dot(mixed.T, basis, precision=hp)
        image = direction + 2.0 / LEAF * near + far
        curvature = lax.psum(jnp.sum(direction * image, axis=1), ("leaf", "sub"))
        step_size = norm_now / curvature
        solution = solution + step_size[:, None] * direction
        residual = residual - step_size[:, None] * image
        norm_next = column_norms(residual)
        direction = residual + (norm_next / norm_now)[:, None] * direction
        norm_now = norm_next
    return (solution, residual)


def solution(mesh):
    in_specs = (
        P(None, ("leaf", "sub")),
        P(None, ("leaf", "sub")),
        P(None, ("leaf", "sub")),
        P(),
        P(("leaf", "sub"), None),
        P(("leaf", "sub")),
    )
    out_specs = (P(None, ("leaf", "sub")), P(None, ("leaf", "sub")))
    return jax.shard_map(body, mesh=mesh, in_specs=in_specs, out_specs=out_specs, check_vma=False)
```

profile of v0, /device:TPU:1, one launch (start us, length us, event | category | flops | bytes accessed | tf_op | source)
XLA Modules:
  0.0 856.1 jit_solution(837808076206261872)
XLA Ops:
  5.2 8.2 collective-permute-start.3
  15.0 7.3 collective-permute-start.8
  24.6 7.3 collective-permute-start.4
  43.2 66.0 %while.36 = (s32[]{:T(128)}, f32[8,64,256]{2,0,1:T(8,128)S(1)}, f32[8,8,64,256]{3,1,0,2:T(8,128)}, s32[8,8]{1,0:T(8,128)S(1)}, bf16[24,64,256]{2,1,0:T(8,128)(2,...) while((s32[]{:T(128)}, f32[8,64,256]{2,0,1:T(8,128)S(1)}, ...), condition=%wide.region_7.8_spmd, body=%wide.region_4.7_spmd.sunk | while | flops 152011808 | bytes 10838393 | solution.py:104
  120.6 4.6 collective-permute-done.13
  134.2 81.5 %all-reduce = (f32[64]{0:T(128)S(1)}, f32[64]{0:T(128)S(1)}) all-reduce(f32[64]{0:T(128)S(1)} %get-tuple-element.188, f32[64]{0:T(128)S(1)} %get-tuple-element.187), channel_id=1, replica_groups=mesh['leaf'=128,'sub'=2] {'leaf','sub'}, use_global_device_ids=true, to_apply=%region_1.2 | all-reduce | flops 128 | bytes 1024 | tf_op jit(solution)/shard_map/psum | solution.py:46
  216.0 74.5 %psum.44 = f32[64]{0:T(128)S(1)} all-reduce(f32[64]{0:T(128)S(1)} %multiply_reduce_fusion.9), channel_id=1, replica_groups=mesh['leaf'=128,'sub'=2] {'leaf','sub'}, use_global_device_ids=true, to_apply=%region_11.12 | all-reduce | flops 64 | bytes 512 | tf_op jit(solution)/shard_map/psum | solution.py:46
  293.9 4.3 collective-permute-done.17
  303.4 103.5 %while.37 = (s32[]{:T(128)}, f32[8,64,256]{2,0,1:T(8,128)}, f32[8,8,64,256]{3,1,0,2:T(8,128)}, s32[8,8]{1,0:T(8,128)S(1)}, bf16[24,64,256]{2,1,0:T(8,128)(2,1)},...) while((s32[]{:T(128)}, f32[8,64,256]{2,0,1:T(8,128)}, ...), condition=%wide.region_15.16_spmd, body=%wide.region_12.15_spmd.sunk | while | flops 152011808 | bytes 10838901 | solution.py:104
  412.8 6.7 collective-permute-start.18
  420.1 7.2 collective-permute-start.20
  434.7 7.0 collective-permute-done.23
  444.7 4.3 collective-permute-done.25
  452.3 4.2 collective-permute-done.27
  457.5 77.9 %psum.45 = f32[64]{0:T(128)S(1)} all-reduce(f32[64]{0:T(128)S(1)} %get-tuple-element.283), channel_id=1, replica_groups=mesh['leaf'=128,'sub'=2] {'leaf','sub'}, use_global_device_ids=true, to_apply=%region_17.18 | all-reduce | flops 64 | bytes 512 | tf_op jit(solution)/shard_map/psum | solution.py:120
  535.7 74.5 %psum.46 = f32[64]{0:T(128)S(1)} all-reduce(f32[64]{0:T(128)S(1)} %get-tuple-element.255), channel_id=1, replica_groups=mesh['leaf'=128,'sub'=2] {'leaf','sub'}, use_global_device_ids=true, to_apply=%region_19.20 | all-reduce | flops 64 | bytes 512 | tf_op jit(solution)/shard_map/psum | solution.py:46
  612.8 4.3 collective-permute-done.29
  622.3 103.7 %while.38 = (s32[]{:T(128)}, f32[8,64,256]{2,0,1:T(8,128)}, f32[8,8,64,256]{3,1,0,2:T(8,128)}, s32[8,8]{1,0:T(8,128)S(1)}, bf16[24,64,256]{2,1,0:T(8,128)(2,1)},...) while((s32[]{:T(128)}, f32[8,64,256]{2,0,1:T(8,128)}, ...), condition=%wide.region_23.24_spmd, body=%wide.region_20.23_spmd.sunk | while | flops 152011808 | bytes 10838901 | solution.py:104
  731.9 6.9 collective-permute-start.30
  739.4 7.2 collective-permute-start.32
  753.9 7.0 collective-permute-done.35
  763.9 4.3 collective-permute-done.37
  771.4 4.2 collective-permute-done.39
  776.5 77.9 %psum.47 = f32[64]{0:T(128)S(1)} all-reduce(f32[64]{0:T(128)S(1)} %get-tuple-element.287), channel_id=1, replica_groups=mesh['leaf'=128,'sub'=2] {'leaf','sub'}, use_global_device_ids=true, to_apply=%region_25.26 | all-reduce | flops 64 | bytes 512 | tf_op jit(solution)/shard_map/psum | solution.py:120
  (607 shorter events, 371.8 us)
Async XLA Ops:
  1.9 38.5 %collective-permute-start.1 = (bf16[8,64,256]{2,0,1:T(8,128)(2,1)S(1)}, bf16[8,64,256]{2,0,1:T(8,128)(2,1)S(1)}, u32[]{:S(2)}, u32[]{:S(2)}) collective-permute-start(bf16[8,64,256]{2,0,1:T(8,128)(2,1)S(1)} %bitcast.234), channel_id=1, source_target_pairs={{0,255},{1,0},{2,1},{3,2},{4,3},{5,4},{6,5},{7,6},{8,7},{9,8},{10,... | collective-permute-start | bytes 786440 | tf_op jit(solution)/shard_map/ppermute | solution.py:13
  5.2 35.2 %collective-permute-start = (bf16[8,64,256]{2,0,1:T(8,128)(2,1)S(1)}, bf16[8,64,256]{2,0,1:T(8,128)(2,1)S(1)}, u32[]{:S(2)}, u32[]{:S(2)}) collective-permute-start(bf16[8,64,256]{2,0,1:T(8,128)(2,1)S(1)} %bitcast.235), channel_id=1, source_target_pairs={{0,1},{1,2},{2,3},{3,4},{4,5},{5,6},{6,7},{7,8},{8,9},{9,10},{10,1... | collective-permute-start | bytes 786440 | tf_op jit(solution)/shard_map/ppermute | solution.py:13
  5.2 30.4 %collective-permute-start.3 = (f32[8,3,256]{2,1,0:T(4,128)}, f32[8,3,256]{2,1,0:T(4,128)S(1)}, u32[]{:S(2)}, u32[]{:S(2)}) collective-permute-start(f32[8,3,256]{2,1,0:T(4,128)} %bitcast.35), channel_id=1, source_target_pairs={{0,255},{1,0},{2,1},{3,2},{4,3},{5,4},{6,5},{7,6},{8,7},{9,8},{10,... | collective-permute-start | bytes 73736 | tf_op jit(solution)/shard_map/ppermute | solution.py:13
  13.4 22.7 %collective-permute-start.2 = (f32[8,3,256]{2,1,0:T(4,128)}, f32[8,3,256]{2,1,0:T(4,128)S(1)}, u32[]{:S(2)}, u32[]{:S(2)}) collective-permute-start(f32[8,3,256]{2,1,0:T(4,128)} %bitcast.35), channel_id=1, source_target_pairs={{0,1},{1,2},{2,3},{3,4},{4,5},{5,6},{6,7},{7,8},{8,9},{9,10},{10,1... | collective-permute-start | bytes 73736 | tf_op jit(solution)/shard_map/ppermute | solution.py:13
  15.0 8.4 collective-permute-start.8
  24.6 8.1 collective-permute-start.4
  39.9 77.1 %collective-permute-start.11 = (f32[64,64]{1,0:T(8,128)}, f32[64,64]{1,0:T(8,128)}, u32[]{:S(2)}, u32[]{:S(2)}) collective-permute-start(f32[64,64]{1,0:T(8,128)} %add.324), channel_id=1, source_target_pairs={{0,8},{2,10},{4,12},{6,14},{8,0},{10,2},{12,4},{14,6},{16,24},{18,... | collective-permute-start | bytes 49160 | tf_op jit(solution)/shard_map/ppermute | solution.py:19
  113.8 15.7 %collective-permute-start.7 = (bf16[8,64,256]{2,0,1:T(8,128)(2,1)S(1)}, bf16[8,64,256]{2,0,1:T(8,128)(2,1)S(1)}, u32[]{:S(2)}, u32[]{:S(2)}) collective-permute-start(bf16[8,64,256]{2,0,1:T(8,128)(2,1)S(1)} %get-tuple-element.264), channel_id=1, source_target_pairs={{0,1},{1,2},{2,3},{3,4},{4,5},{5,6},{6,7},{7,8},{8,9},{9,10},{10,1... | collective-permute-start | bytes 786440 | tf_op jit(solution)/shard_map/ppermute | solution.py:13
  116.2 13.3 %collective-permute-start.6 = (bf16[8,64,256]{2,0,1:T(8,128)(2,1)S(1)}, bf16[8,64,256]{2,0,1:T(8,128)(2,1)S(1)}, u32[]{:S(2)}, u32[]{:S(2)}) collective-permute-start(bf16[8,64,256]{2,0,1:T(8,128)(2,1)S(1)} %get-tuple-element.263), channel_id=1, source_target_pairs={{0,255},{1,0},{2,1},{3,2},{4,3},{5,4},{6,5},{7,6},{8,7},{9,8},{10,... | collective-permute-start | bytes 786440 | tf_op jit(solution)/shard_map/ppermute | solution.py:13
  120.6 4.6 collective-permute-start.13
  292.0 6.2 collective-permute-start.17
  292.8 5.3 collective-permute-start.16
  411.0 40.9 %collective-permute-start.19 = (bf16[8,64,256]{2,0,1:T(8,128)(2,1)S(1)}, bf16[8,64,256]{2,0,1:T(8,128)(2,1)S(1)}, u32[]{:S(2)}, u32[]{:S(2)}) collective-permute-start(bf16[8,64,256]{2,0,1:T(8,128)(2,1)S(1)} %get-tuple-element.262), channel_id=1, source_target_pairs={{0,1},{1,2},{2,3},{3,4},{4,5},{5,6},{6,7},{7,8},{8,9},{9,10},{10,1... | collective-permute-start | bytes 786440 | tf_op jit(solution)/shard_map/ppermute | solution.py:13
  412.8 39.1 %collective-permute-start.18 = (bf16[8,64,256]{2,0,1:T(8,128)(2,1)S(1)}, bf16[8,64,256]{2,0,1:T(8,128)(2,1)S(1)}, u32[]{:S(2)}, u32[]{:S(2)}) collective-permute-start(bf16[8,64,256]{2,0,1:T(8,128)(2,1)S(1)} %get-tuple-element.261), channel_id=1, source_target_pairs={{0,255},{1,0},{2,1},{3,2},{4,3},{5,4},{6,5},{7,6},{8,7},{9,8},{10,... | collective-permute-start | bytes 786440 | tf_op jit(solution)/shard_map/ppermute | solution.py:13
  420.1 8.0 collective-permute-start.20
  434.7 7.0 collective-permute-start.23
  451.9 4.6 collective-permute-start.27
  611.1 6.0 collective-permute-start.29
  611.7 5.3 collective-permute-start.28
  730.1 40.9 %collective-permute-start.31 = (bf16[8,64,256]{2,0,1:T(8,128)(2,1)S(1)}, bf16[8,64,256]{2,0,1:T(8,128)(2,1)S(1)}, u32[]{:S(2)}, u32[]{:S(2)}) collective-permute-start(bf16[8,64,256]{2,0,1:T(8,128)(2,1)S(1)} %get-tuple-element.260), channel_id=1, source_target_pairs={{0,1},{1,2},{2,3},{3,4},{4,5},{5,6},{6,7},{7,8},{8,9},{9,10},{10,1... | collective-permute-start | bytes 786440 | tf_op jit(solution)/shard_map/ppermute | solution.py:13
  731.9 39.1 %collective-permute-start.30 = (bf16[8,64,256]{2,0,1:T(8,128)(2,1)S(1)}, bf16[8,64,256]{2,0,1:T(8,128)(2,1)S(1)}, u32[]{:S(2)}, u32[]{:S(2)}) collective-permute-start(bf16[8,64,256]{2,0,1:T(8,128)(2,1)S(1)} %get-tuple-element.259), channel_id=1, source_target_pairs={{0,255},{1,0},{2,1},{3,2},{4,3},{5,4},{6,5},{7,6},{8,7},{9,8},{10,... | collective-permute-start | bytes 786440 | tf_op jit(solution)/shard_map/ppermute | solution.py:13
  739.4 8.0 collective-permute-start.32
  753.9 7.0 collective-permute-start.35
  771.0 4.6 collective-permute-start.39
  (59 other events, 1282.8 us)
where the time goes:
time: 867 us; the launch traced here: 856 us
  blocking collectives  386 us (45%)
  local copies, waits for them, and re-layouts  176 us (20%)
  waiting for transfers between devices  85.6 us (10%)
  matrix products  80.2 us (9%)
  starting transfers between devices  66.6 us (8%)
  other arithmetic  58.5 us (7%)
    psum x3, blocking collectives, column_norms(): return lax.psum(jnp.sum(field * field, axis=1), ('leaf', 'sub'))  231 us
    psum x2, blocking collectives, body(): curvature = lax.psum(jnp.sum(direction * image, axis=1), ('leaf', 'sub'))  156 us
    ppermute x24, waiting for transfers between devices, partner_2(): return lax.ppermute(value, axis, pairs)  75.1 us
    dynamic_update_slice x72, local copies, waits for them, and re-layouts, body(): lax.map(leaf_work, (coords, rounded, local_slot, active, self_weight))  74.6 us
    ppermute x16, starting transfers between devices, shifted(): lax.ppermute(shard, axis, [(i, (i + by) % peers) for i in range(peers)])  43 us
    dot_general x24, matrix products, leaf_work(): jnp.einsum('cb,ab->ca', leaf_vals, own_tile, preferred_element_type=jnp.f...  32.4 us
    gather x24, local copies, waits for them, and re-layouts, leaf_work(): part_vals = pool[leaf_slots]  31.6 us
    mul x24, other arithmetic, leaf_work(): kernel(leaf_pts[None], part_pts).astype(jnp.bfloat16)  27.3 us
  transfers between devices with their start and end apart: 40, of which 26 were waited for; matrix products, arithmetic and copies ran while one was open for 9% of the time, Pallas kernels for 0%

commit v1 on v0

v1 whole, which is shorter than its diff:
```python
import math
import jax
import jax.numpy as jnp
from jax import lax
from jax.experimental import pallas as pl
from jax.experimental.pallas import tpu as pltpu
from jax.sharding import PartitionSpec as P

LEAF = 256
NEAR = 8
MESH = pl.DeviceIdType.MESH
F32 = jnp.float32
BF16 = jnp.bfloat16
SCALE = math.sqrt(3.0) / 0.08 * math.log2(math.e)
LN2 = math.log(2.0)
RING_HOPS = (0, 1, 2, 1)
Z_MASKS = (8, 10, 6, 12, 14, 4, 2)
XY_MASKS = tuple(
    sorted(range(16, 256, 16), key=lambda m: -(RING_HOPS[(m >> 4) & 3] + RING_HOPS[m >> 6]))
)
N_Z = len(Z_MASKS)
N_XY = len(XY_MASKS)


def level_of(mask):
    return mask.bit_length()


def split2(value):
    high = value.astype(BF16)
    return high, (value - high.astype(F32)).astype(BF16)


def split3(value):
    high = value.astype(BF16).astype(F32)
    rest = value - high
    mid = rest.astype(BF16).astype(F32)
    low = (rest - mid).astype(BF16).astype(F32)
    return high, mid, low


def kernel(
    rhs, pts, basis, dec, lists, x_out, r_out,
    tiles, own_tiles, left_feat, right_feat, stage, gathered, pool0, pool1, pool2, near, basis2, stacked,
    b0, y1, r1, b1, y2, side_pts, side_lists, table_v, table,
    src, sib_in, z_in, xy_in, last_src, last_sib, last_z, last_xy,
    side_ss, side_rs, sib_ss, sib_rs, z_ss, z_rs, xy_ss, xy_rs, table_sem,
):
    nleaf = rhs.shape[1] // LEAF
    pool = (pool0, pool1, pool2)
    me = lax.axis_index("leaf") * 2 + lax.axis_index("sub")
    ndev = 256

    def at(index):
        return (index // 2, lax.rem(index, 2))

    def peer(mask):
        return at(jnp.bitwise_xor(me, mask))

    prev, following = lax.rem(me + ndev - 1, ndev), lax.rem(me + 1, ndev)
    barrier = pltpu.get_barrier_semaphore()
    everyone = [at(prev), at(following), peer(1)] + [peer(m) for m in Z_MASKS + XY_MASKS]
    for other in everyone:
        pl.semaphore_signal(barrier, inc=1, device_id=other, device_id_type=MESH)

    def send(source, target, send_sem, recv_sem, device):
        copy = pltpu.make_async_remote_copy(
            src_ref=source, dst_ref=target, send_sem=send_sem, recv_sem=recv_sem,
            device_id=device, device_id_type=MESH,
        )
        copy.start()
        return copy

    def cols(g):
        return slice(g * LEAF, (g + 1) * LEAF)

    def put_pool(step, g, value):
        pool[step][nleaf + g] = value.astype(BF16)

    def send_sides(step):
        own = pool[step].at[nleaf : 2 * nleaf]
        return [
            send(own, pool[step].at[0:nleaf], side_ss.at[step, 0], side_rs.at[step, 0], at(following)),
            send(own, pool[step].at[2 * nleaf :], side_ss.at[step, 1], side_rs.at[step, 1], at(prev)),
        ]

    lane = lax.broadcasted_iota(jnp.int32, (32, 128), 1)
    low_half = lane < 64
    row16 = lax.broadcasted_iota(jnp.int32, (16, 128), 0)
    row64 = lax.broadcasted_iota(jnp.int32, (64, 128), 0)
    col64 = lax.broadcasted_iota(jnp.int32, (64, 128), 1)

    def to_row(first, second):
        spread = jnp.where(col64 == row64, first, 0.0) + jnp.where(col64 == row64 + 64, second, 0.0)
        return jnp.sum(spread, axis=0, keepdims=True)

    def from_row(row):
        first = jnp.sum(jnp.where(col64 == row64, row, 0.0), axis=1, keepdims=True)
        second = jnp.sum(jnp.where(col64 == row64 + 64, row, 0.0), axis=1, keepdims=True)
        return first, second

    def fold(value):
        return value[:, 0:128] + value[:, 128:256]

    def lanes(value):
        return jnp.sum(value, axis=1, keepdims=True)

    weights = [None, dec[0:1, :]]
    for _ in range(7):
        weights.append(weights[-1] * dec[0:1, :] * math.sqrt(0.5))

    def coeffs(field):
        for g in range(nleaf):
            high, low = split2(field[:, cols(g)])
            stacked[0:64, cols(g)] = high
            stacked[64:128, cols(g)] = low
        full = lax.dot_general(
            stacked[...], basis2[...], (((1,), (1,)), ((), ())), preferred_element_type=F32
        )
        total = full[0:64, 0:128] + full[64:128, 0:128] + full[0:64, 128:256]
        return jnp.where(low_half, total[0:32], total[32:64])

    def write_message(slot, coef, scalars):
        high, mid, low = split3(scalars)
        rows = jnp.where(row16 == 0, high, jnp.where(row16 == 1, mid, jnp.where(row16 == 2, low, 0.0)))
        src[slot, 0:32] = coef.astype(BF16)
        src[slot, 32:48] = rows.astype(BF16)

    def read_message(ref):
        return ref[0:32].astype(F32), jnp.sum(ref[32:48].astype(F32), axis=0, keepdims=True)

    def start_sib(step, coef, scalars):
        write_message(3 * step, coef, scalars)
        return send(src.at[3 * step], sib_in.at[step], sib_ss.at[step], sib_rs.at[step], peer(1))

    def start_z(step, copy, coef, scalars):
        copy.wait()
        other, other_scalars = read_message(sib_in.at[step])
        mixed = coef + weights[1] * other
        total, scalars = coef + other, scalars + other_scalars
        write_message(3 * step + 1, total, scalars)
        copies = [
            send(src.at[3 * step + 1], z_in.at[step, k], z_ss.at[step, k], z_rs.at[step, k], peer(m))
            for k, m in enumerate(Z_MASKS)
        ]
        return copies, mixed, total, scalars

    def collect(copies, masks, buffer, mixed, total, scalars):
        for copy in copies:
            copy.wait()
        levels = {}
        for k, mask in enumerate(masks):
            other, other_scalars = read_message(buffer.at[k])
            level = level_of(mask)
            levels[level] = other if level not in levels else levels[level] + other
            scalars = scalars + other_scalars
        for level, other in levels.items():
            mixed = mixed + weights[level] * other
            total = total + other
        return mixed, total, scalars

    def start_xy(step, copies, mixed, total, scalars):
        mixed, total, scalars = collect(copies, Z_MASKS, z_in.at[step], mixed, total, scalars)
        write_message(3 * step + 2, total, scalars)
        copies = [
            send(src.at[3 * step + 2], xy_in.at[step, k], xy_ss.at[step, k], xy_rs.at[step, k], peer(m))
            for k, m in enumerate(XY_MASKS)
        ]
        return copies, mixed, total, scalars

    def finish(step, copies, mixed, total, scalars):
        mixed, _, scalars = collect(copies, XY_MASKS, xy_in.at[step], mixed, total, scalars)
        both = jnp.concatenate(
            [jnp.where(low_half, mixed, 0.0), jnp.where(low_half, 0.0, mixed)], axis=0
        )
        high, low = split2(both)
        return jnp.concatenate([high, high], axis=1), low, scalars

    def image(g, wide, low):
        far = jnp.dot(wide, basis2[:, cols(g)], preferred_element_type=F32)
        far = far + jnp.dot(low, basis2[0:128, cols(g)], preferred_element_type=F32)
        return near[g] * (2.0 / LEAF) + far

    high, low = split2(basis[...])
    basis2[0:64] = high
    basis2[64:128] = high
    basis2[128:192] = low
    basis2[192:256] = low
    for g in range(nleaf):
        put_pool(0, g, rhs[:, cols(g)])
    coef = coeffs(rhs)
    none = jnp.zeros((1, 128), F32)
    pl.semaphore_wait(barrier, len(everyone))

    side = [
        send(pts, side_pts.at[0], side_ss.at[3, 0], side_rs.at[3, 0], at(following)),
        send(pts, side_pts.at[1], side_ss.at[3, 1], side_rs.at[3, 1], at(prev)),
        send(lists, side_lists.at[0], side_ss.at[4, 0], side_rs.at[4, 0], at(following)),
        send(lists, side_lists.at[1], side_ss.at[4, 1], side_rs.at[4, 1], at(prev)),
    ]
    sib = start_sib(0, coef, none)
    values = send_sides(0)

    center = pts[:, 0:1]
    row8 = lax.broadcasted_iota(jnp.int32, (8, nleaf * LEAF), 0)

    def parts(coords):
        scaled = (coords - center) * SCALE
        norm = jnp.sum(scaled * scaled, axis=0, keepdims=True)
        return split3(scaled), norm

    def left(coords, first):
        (one, two, three), norm = parts(coords)
        n1, n2, n3 = split3(norm + SCALE * SCALE * 0.0001)
        ends = jnp.where(row8 < 6, 1.0, 0.0)
        ends = jnp.where(row8 == 0, n1, jnp.where(row8 == 1, n2, jnp.where(row8 == 2, n3, ends)))
        for k, block in enumerate((one, one, two, two, one, three, ends)):
            stage[8 * k : 8 * k + 8, :] = block
        for g in range(nleaf):
            left_feat[first + g] = jnp.transpose(stage[:, cols(g)]).astype(BF16)

    def right(coords):
        (one, two, three), norm = parts(coords)
        n1, n2, n3 = split3(norm)
        ends = jnp.where(row8 < 3, 1.0, 0.0)
        ends = jnp.where(row8 == 3, n1, jnp.where(row8 == 4, n2, jnp.where(row8 == 5, n3, ends)))
        one, two, three = -2.0 * one, -2.0 * two, -2.0 * three
        for k, block in enumerate((one, two, one, two, three, one, ends)):
            stage[8 * k : 8 * k + 8, :] = block
        for g in range(nleaf):
            right_feat[g] = stage[:, cols(g)].astype(BF16)

    stage[56:, :] = jnp.zeros((stage.shape[0] - 56, nleaf * LEAF), F32)
    right(pts[...])
    left(pts[...], nleaf)

    def tile(leaf, g, one, slope):
        square = jnp.dot(left_feat[leaf], right_feat[g], preferred_element_type=F32)
        root = square * lax.rsqrt(square)
        return (jnp.exp2(-root) * (one + slope * root)).astype(BF16)

    z, mixed, total, scalars = start_z(0, sib, coef, none)

    def self_tile(g, carry):
        own_tiles[g] = tile(nleaf + g, g, 1.0, LN2)
        return carry

    lax.fori_loop(0, nleaf, self_tile, 0)

    for copy in side:
        copy.wait()
    left(side_pts[0], 0)
    left(side_pts[1], 2 * nleaf)

    row = lax.broadcasted_iota(jnp.int32, (8, 128), 0)
    slot = lax.broadcasted_iota(jnp.int32, (8, 128), 1)
    mine = lists[...]
    counts = mine[:, NEAR : NEAR + 1]
    place = jnp.bitwise_and(jnp.right_shift(mine, 3) - me + 1, ndev - 1)
    index = jnp.clip(place * nleaf + jnp.bitwise_and(mine, nleaf - 1), 0, 3 * nleaf - 1)
    table_v[0] = index
    table_v[2] = (slot < counts).astype(jnp.int32)
    named = jnp.zeros((8, 128), jnp.int32)
    named_active = jnp.zeros((8, 128), jnp.int32)
    for k, theirs in enumerate((side_lists[0], mine, side_lists[1])):
        live = (slot < theirs[:, NEAR : NEAR + 1]).astype(jnp.int32)
        for g in range(nleaf):
            match = theirs == me * nleaf + g
            where = jnp.sum(jnp.where(match, row + k * nleaf, 0), axis=0, keepdims=True)
            alive = jnp.sum(jnp.where(match, live, 0), axis=0, keepdims=True)
            named = named + jnp.where(row == g, where, 0)
            named_active = named_active + jnp.where(row == g, alive, 0)
    table_v[1] = jnp.clip(named, 0, 3 * nleaf - 1)
    table_v[3] = named_active
    times = counts + jnp.sum(jnp.where(slot < NEAR, named_active, 0), axis=1, keepdims=True)
    table_v[4] = jnp.broadcast_to(times, (8, 128))
    to_table = pltpu.make_async_copy(table_v, table, table_sem)
    to_table.start()
    to_table.wait()

    def apply_near(step, g):
        for k in range(NEAR):
            gathered[:, k * LEAF : (k + 1) * LEAF] = pool[step][table[0, g, k]]
            gathered[:, (NEAR + k) * LEAF : (NEAR + k + 1) * LEAF] = pool[step][table[1, g, k]]
        others = jnp.dot(gathered[...], tiles[g], preferred_element_type=F32)
        own = jnp.dot(pool[step][nleaf + g], own_tiles[g], preferred_element_type=F32)
        near[g] = others + table[4, g, 0].astype(F32) * own

    for copy in values:
        copy.wait()
    xy, mixed, total, scalars = start_xy(0, z, mixed, total, scalars)

    def first_near(g, carry):
        def half(h, carry):
            for k in range(NEAR):
                one = table[2 + h, g, k].astype(F32)
                value = tile(table[h, g, k], g, one, one * LN2)
                tiles[g, pl.ds(pl.multiple_of((h * NEAR + k) * LEAF, LEAF), LEAF), :] = value
            return carry

        lax.fori_loop(0, 2, half, 0)
        apply_near(0, g)
        return carry

    lax.fori_loop(0, nleaf, first_near, 0)

    def later_near(step, values):
        for copy in values:
            copy.wait()

        def one_leaf(g, carry):
            apply_near(step, g)
            return carry

        lax.fori_loop(0, nleaf, one_leaf, 0)

    wide, low, _ = finish(0, xy, mixed, total, scalars)
    rr = jnp.zeros((64, 128), F32)
    rb = jnp.zeros((64, 128), F32)
    for g in range(nleaf):
        value = image(g, wide, low)
        b0[:, cols(g)] = value
        put_pool(1, g, value)
        held = rhs[:, cols(g)]
        rr = rr + fold(held * held)
        rb = rb + fold(held * value)
    values = send_sides(1)
    scalars = to_row(lanes(rr), lanes(rb))
    coef = coeffs(b0)
    sib = start_sib(1, coef, scalars)
    z, mixed, total, scalars = start_z(1, sib, coef, scalars)
    xy, mixed, total, scalars = start_xy(1, z, mixed, total, scalars)
    later_near(1, values)

    wide, low, scalars = finish(1, xy, mixed, total, scalars)
    rr0, rb0 = from_row(scalars)
    alpha0 = rr0 / (rr0 + rb0)
    rr = jnp.zeros((64, 128), F32)
    rb = jnp.zeros((64, 128), F32)
    for g in range(nleaf):
        value = image(g, wide, low)
        y1[:, cols(g)] = value
        one = b0[:, cols(g)]
        held = rhs[:, cols(g)]
        res = held - alpha0 * (held + one)
        nxt = one - alpha0 * (one + value)
        r1[:, cols(g)] = res
        b1[:, cols(g)] = nxt
        put_pool(2, g, nxt)
        rr = rr + fold(res * res)
        rb = rb + fold(res * nxt)
    values = send_sides(2)
    scalars = to_row(lanes(rr), lanes(rb))
    coef = coeffs(b1)
    sib = start_sib(2, coef, scalars)
    z, mixed, total, scalars = start_z(2, sib, coef, scalars)
    xy, mixed, total, scalars = start_xy(2, z, mixed, total, scalars)
    later_near(2, values)

    wide, low, scalars = finish(2, xy, mixed, total, scalars)
    rr1, rb1 = from_row(scalars)
    beta0 = rr1 / rr0
    alpha1 = rr1 / (rr1 + rb1 - beta0 * rr1 / alpha0)
    rr = jnp.zeros((64, 128), F32)
    rb = jnp.zeros((64, 128), F32)
    for g in range(nleaf):
        value = image(g, wide, low) + beta0 * y1[:, cols(g)]
        direction = r1[:, cols(g)] + beta0 * rhs[:, cols(g)]
        moved = b1[:, cols(g)] + beta0 * b0[:, cols(g)]
        res = r1[:, cols(g)] - alpha1 * (direction + moved)
        nxt = b1[:, cols(g)] - alpha1 * (moved + value)
        y1[:, cols(g)] = direction
        b0[:, cols(g)] = moved
        y2[:, cols(g)] = nxt
        r1[:, cols(g)] = res
        rr = rr + fold(res * res)
        rb = rb + fold(res * nxt)
    scalars = to_row(lanes(rr), lanes(rb))

    last_src[0] = jnp.broadcast_to(scalars, (8, 128))
    copy = send(last_src.at[0], last_sib, sib_ss.at[3], sib_rs.at[3], peer(1))
    copy.wait()
    scalars = scalars + last_sib[0:1]
    for stage_num, (masks, buffer, ss, rs) in enumerate(
        ((Z_MASKS, last_z, z_ss, z_rs), (XY_MASKS, last_xy, xy_ss, xy_rs))
    ):
        last_src[1 + stage_num] = jnp.broadcast_to(scalars, (8, 128))
        copies = [
            send(last_src.at[1 + stage_num], buffer.at[k], ss.at[3, k], rs.at[3, k], peer(m))
            for k, m in enumerate(masks)
        ]
        for copy in copies:
            copy.wait()
        for k in range(len(masks)):
            scalars = scalars + buffer[k, 0:1]
    rr2, rb2 = from_row(scalars)
    beta1 = rr2 / rr1
    alpha2 = rr2 / (rr2 + rb2 - beta1 * rr2 / alpha1)
    for g in range(nleaf):
        direction = r1[:, cols(g)] + beta1 * y1[:, cols(g)]
        moved = y2[:, cols(g)] + beta1 * b0[:, cols(g)]
        r_out[:, cols(g)] = r1[:, cols(g)] - alpha2 * (direction + moved)
        x_out[:, cols(g)] = (
            alpha0 * rhs[:, cols(g)] + alpha1 * y1[:, cols(g)] + alpha2 * direction
        )


def body(rhs, points, basis, decay, near_list, near_count):
    nrows, npts = rhs.shape
    nleaf = npts // LEAF
    pts = jnp.pad(points, ((0, 5), (0, 0)))
    lists = jnp.concatenate([near_list, near_count[:, None]], axis=1)
    lists = jnp.pad(lists, ((0, 0), (0, 128 - NEAR - 1)))
    dec = jnp.broadcast_to(jnp.concatenate([decay, decay])[None, :], (8, 128))
    vmem = pl.BlockSpec(memory_space=pltpu.VMEM)
    field = pltpu.VMEM((nrows, npts), F32)
    dma = pltpu.SemaphoreType.DMA
    shape = jax.ShapeDtypeStruct((nrows, npts), F32)
    return pl.pallas_call(
        kernel,
        out_shape=(shape, shape),
        in_specs=[vmem] * 5,
        out_specs=(vmem, vmem),
        scratch_shapes=[
            pltpu.VMEM((nleaf, 2 * NEAR * LEAF, LEAF), BF16),
            pltpu.VMEM((nleaf, LEAF, LEAF), BF16),
            pltpu.VMEM((3 * nleaf, LEAF, 64), BF16),
            pltpu.VMEM((nleaf, 64, LEAF), BF16),
            pltpu.VMEM((64, npts), F32),
            pltpu.VMEM((nrows, 2 * NEAR * LEAF), BF16),
            *[pltpu.VMEM((3 * nleaf, nrows, LEAF), BF16)] * 3,
            pltpu.VMEM((nleaf, nrows, LEAF), F32),
            pltpu.VMEM((256, npts), BF16),
            pltpu.VMEM((128, npts), BF16),
            field, field, field, field, field,
            pltpu.VMEM((2, 8, npts), F32),
            pltpu.VMEM((2, 8, 128), jnp.int32),
            pltpu.VMEM((5, 8, 128), jnp.int32),
            pltpu.SMEM((5, 8, 128), jnp.int32),
            pltpu.VMEM((9, 48, 128), BF16),
            pltpu.VMEM((3, 48, 128), BF16),
            pltpu.VMEM((3, N_Z, 48, 128), BF16),
            pltpu.VMEM((3, N_XY, 48, 128), BF16),
            pltpu.VMEM((3, 8, 128), F32),
            pltpu.VMEM((8, 128), F32),
            pltpu.VMEM((N_Z, 8, 128), F32),
            pltpu.VMEM((N_XY, 8, 128), F32),
            dma((5, 2)), dma((5, 2)), dma((4,)), dma((4,)),
            dma((4, N_Z)), dma((4, N_Z)), dma((4, N_XY)), dma((4, N_XY)),
            dma,
        ],
        compiler_params=pltpu.CompilerParams(
            collective_id=0, has_side_effects=True, vmem_limit_bytes=56 * 2**20
        ),
    )(rhs, pts, basis, dec, lists)


def solution(mesh):
    in_specs = (
        P(None, ("leaf", "sub")),
        P(None, ("leaf", "sub")),
        P(None, ("leaf", "sub")),
        P(),
        P(("leaf", "sub"), None),
        P(("leaf", "sub")),
    )
    out_specs = (P(None, ("leaf", "sub")), P(None, ("leaf", "sub")))
    return jax.shard_map(body, mesh=mesh, in_specs=in_specs, out_specs=out_specs, check_vma=False)
```

time: 867 us -> 86.1 us (0.10); the launches traced: 856 us -> 85.9 us
  blocking collectives: 386 us -> 0 us
  local copies, waits for them, and re-layouts: 176 us -> 5.93 us
  waiting for transfers between devices: 85.6 us -> 0 us
  matrix products: 80.2 us -> 0 us
  Pallas kernels: 0 us -> 78.4 us
  starting transfers between devices: 66.6 us -> 0 us
  other arithmetic: 58.5 us -> 0.83 us
    psum x5 -> x0, blocking collectives: 386 us -> none  [the longest x3 231 us: column_norms(): return lax.psum(jnp.sum(field * field, axis=1), ('leaf', 'sub'))]
    ppermute x40 -> x0, waiting for transfers between devices: 85.6 us -> none  [the longest x24 75.1 us: partner_2(): return lax.ppermute(value, axis, pairs)]
    dot_general x81 -> x0, matrix products: 80.2 us -> none  [the longest x24 32.4 us: leaf_work(): jnp.einsum('cb,ab->ca', leaf_vals, own_tile, preferred_element_type=jnp.f...]
    pallas_call x0 -> x1, Pallas kernels: none -> 78.4 us  [body(): pl.pallas_call(kernel, out_shape=(shape, shape), in_specs=[vmem] * 5, out...]
    dynamic_update_slice x72 -> x0, local copies, waits for them, and re-layouts: 74.6 us -> none  [body(): lax.map(leaf_work, (coords, rounded, local_slot, active, self_weight))]
    ppermute x40 -> x0, starting transfers between devices: 66.6 us -> none  [the longest x16 43 us: shifted(): lax.ppermute(shard, axis, [(i, (i + by) % peers) for i in range(peers)])]
    gather x48 -> x0, local copies, waits for them, and re-layouts: 45.5 us -> none  [the longest x24 31.6 us: leaf_work(): part_vals = pool[leaf_slots]]
    mul x28 -> x0, other arithmetic: 27.8 us -> none  [the longest x24 27.3 us: leaf_work(): kernel(leaf_pts[None], part_pts).astype(jnp.bfloat16)]
  transfers between devices with their start and end apart: 40 -> 0, of which waited for: 26 -> 0; matrix products, arithmetic and copies ran while one was open for 9% -> 0% of each run, Pallas kernels for 0% -> 0%
where the time goes in v1:
time: 86.1 us; the launch traced here: 85.9 us
  Pallas kernels  78.4 us (91%)
  local copies, waits for them, and re-layouts  5.93 us (7%)
    pallas_call x1, Pallas kernels, body(): pl.pallas_call(kernel, out_shape=(shape, shape), in_specs=[vmem] * 5, out...  78.4 us
    unnamed x8, local copies, waits for them, and re-layouts  3.37 us

profile of v1, /device:TPU:1, one launch (start us, length us, event | category | flops | bytes accessed | tf_op | source)
XLA Modules:
  0.0 85.9 jit_solution(2430503806970754835)
XLA Ops:
  0.6 0.0 copy-start.2
  0.6 0.0 copy-start.1
  0.6 0.6 copy-done.2
  1.3 0.1 pad_maximum_fusion
  1.4 0.6 broadcast_in_dim.4.dec
  2.0 0.7 copy.8
  2.7 0.8 pad_add_fusion
  3.4 0.6 pad.9.lists
  4.0 0.0 copy-done.1
  4.0 0.6 pad.8.pts
  4.7 78.4 %shard_map.77 = (f32[64,2048]{1,0:T(8,128)}, f32[64,2048]{1,0:T(8,128)}) custom-call(f32[64,2048]{1,0:T(8,128)} %rhs.1, f32[8,2048]{1,0:T(8,128)} %pad.8.pts, f32[64,2048]{1,0:T(8,128)} %basis.1, f32[8,128]{1,0:T(8,128)} %broadcast_in_dim.4.dec, s32[8,128]{1,0:T(8,128)} %pad.9.lists), custom_call_target="tpu_custom_call" | custom-call | tf_op jit(solution)/shard_map/pallas_call | solution.py:419
  83.1 0.0 copy-start
  83.1 1.9 %copy.11 = f32[64,2048]{1,0:T(8,128)} copy(f32[64,2048]{1,0:T(8,128)} %get-tuple-element.4) | data formatting | bytes 1048576
  85.1 0.0 copy-done
  85.1 0.8 copy.12
Async XLA Ops:
  0.6 0.7 copy-start.2
  0.6 3.4 %copy-start.1 = (f32[3,2048]{1,0:T(4,128)S(1)}, f32[3,2048]{1,0:T(4,128)}, u32[]{:S(2)}) copy-start(f32[3,2048]{1,0:T(4,128)} %param.7) | copy-start | bytes 73732
  83.1 1.9 %copy-start = (f32[64,2048]{1,0:T(8,128)S(1)}, f32[64,2048]{1,0:T(8,128)}, u32[]{:S(2)}) copy-start(f32[64,2048]{1,0:T(8,128)} %get-tuple-element.5) | copy-start | bytes 1572868

commit v2 on v1

v2 whole, which is shorter than its diff:
```python
import math
import jax
import jax.numpy as jnp
from jax import lax
from jax.experimental import pallas as pl
from jax.experimental.pallas import tpu as pltpu
from jax.sharding import PartitionSpec as P

LEAF = 256
NEAR = 8
MESH = pl.DeviceIdType.MESH
F32 = jnp.float32
BF16 = jnp.bfloat16
SCALE = math.sqrt(3.0) / 0.08 * math.log2(math.e)
LN2 = math.log(2.0)
RING_HOPS = (0, 1, 2, 1)
Z_MASKS = (8, 10, 6, 12, 14, 4, 2)
XY_MASKS = tuple(
    sorted(range(16, 256, 16), key=lambda m: -(RING_HOPS[(m >> 4) & 3] + RING_HOPS[m >> 6]))
)
N_Z = len(Z_MASKS)
N_XY = len(XY_MASKS)


def level_of(mask):
    return mask.bit_length()


def split2(value):
    high = value.astype(BF16)
    return high, (value - high.astype(F32)).astype(BF16)


def split3(value):
    high = value.astype(BF16).astype(F32)
    rest = value - high
    mid = rest.astype(BF16).astype(F32)
    low = (rest - mid).astype(BF16).astype(F32)
    return high, mid, low


def kernel(
    rhs, pts, basis, decay, near_list, near_count, x_out, r_out,
    tiles, own_tiles, left_feat, right_feat, stage, gathered, pool0, pool1, pool2, near,
    basis2, stacked, gram, b0, y1, r1, b1, r2, b2, lists, side_pts, side_lists, table_v, table,
    part_src0, part_src1, part_in0, part_in1, side_basis, coef_src, coef_in,
    src, sib_in, z_in, xy_in, last_src, last_sib, last_z, last_xy,
    side_ss, side_rs, sib_ss, sib_rs, z_ss, z_rs, xy_ss, xy_rs, part_ss, part_rs,
    basis_ss, basis_rs, coef_ss, coef_rs, table_sem,
):
    nleaf = rhs.shape[1] // LEAF
    pool = (pool0, pool1, pool2)
    part_src = (part_src0, part_src1)
    part_in = (part_in0, part_in1)
    scale = 2.0 / LEAF
    me = lax.axis_index("leaf") * 2 + lax.axis_index("sub")
    ndev = 256

    def at(index):
        return (index // 2, lax.rem(index, 2))

    def peer(mask):
        return at(jnp.bitwise_xor(me, mask))

    prev, following = lax.rem(me + ndev - 1, ndev), lax.rem(me + 1, ndev)
    barrier = pltpu.get_barrier_semaphore()
    everyone = [peer(m) for m in Z_MASKS + XY_MASKS] + [at(prev), at(following), peer(1)]
    for other in everyone:
        pl.semaphore_signal(barrier, inc=1, device_id=other, device_id_type=MESH)

    def send(source, target, send_sem, recv_sem, device):
        copy = pltpu.make_async_remote_copy(
            src_ref=source, dst_ref=target, send_sem=send_sem, recv_sem=recv_sem,
            device_id=device, device_id_type=MESH,
        )
        copy.start()
        return copy

    def cols(g):
        return slice(g * LEAF, (g + 1) * LEAF)

    def put_pool(step, g, value):
        pool[step][nleaf + g] = value.astype(BF16)

    def both_ways(source, targets, send_sems, recv_sems):
        return [
            send(source, targets[0], send_sems[0], recv_sems[0], at(following)),
            send(source, targets[1], send_sems[1], recv_sems[1], at(prev)),
        ]

    def part_copies(step, leaves):
        return [
            pltpu.make_async_remote_copy(
                src_ref=part_src[step].at[leaves], dst_ref=part_in[step].at[side, leaves],
                send_sem=part_ss.at[step, side], recv_sem=part_rs.at[step, side],
                device_id=device, device_id_type=MESH,
            )
            for side, device in enumerate((at(following), at(prev)))
        ]

    def start_part(step, g):
        for copy in part_copies(step, g):
            copy.start()

    def send_coef(step, packed):
        coef_src[step] = packed.astype(BF16)
        return both_ways(
            coef_src.at[step], (coef_in.at[step, 0], coef_in.at[step, 1]),
            (coef_ss.at[step, 0], coef_ss.at[step, 1]), (coef_rs.at[step, 0], coef_rs.at[step, 1]),
        )

    def side_images(step, copies, combine):
        for copy in copies:
            copy.wait()
        for copy in part_copies(step, slice(0, nleaf)):
            copy.wait()
        for side in range(2):
            packed = coef_in[step, side].astype(F32)
            turned = pltpu.roll(packed, 64, 1)
            narrow = jnp.concatenate([packed[:, 0:64], turned[:, 0:64]], axis=0).astype(BF16)
            for g in range(nleaf):
                part = jnp.dot(narrow, side_basis[side, :, cols(g)], preferred_element_type=F32)
                leaf = 2 * nleaf * side + g
                value = part_in[step][side, g].astype(F32) + part
                pool[step + 1][leaf] = combine(leaf, value).astype(BF16)

    lane = lax.broadcasted_iota(jnp.int32, (32, 128), 1)
    low_half = lane < 64
    row16 = lax.broadcasted_iota(jnp.int32, (16, 128), 0)
    row64 = lax.broadcasted_iota(jnp.int32, (64, 128), 0)
    col64 = lax.broadcasted_iota(jnp.int32, (64, 128), 1)

    def to_row(first, second):
        spread = jnp.where(col64 == row64, first, 0.0) + jnp.where(col64 == row64 + 64, second, 0.0)
        return jnp.sum(spread, axis=0, keepdims=True)

    def from_row(row):
        first = jnp.sum(jnp.where(col64 == row64, row, 0.0), axis=1, keepdims=True)
        second = jnp.sum(jnp.where(col64 == row64 + 64, row, 0.0), axis=1, keepdims=True)
        return first, second

    def fold(value):
        return value[:, 0:128] + value[:, 128:256]

    def lanes(value):
        return jnp.sum(value, axis=1, keepdims=True)

    def pack(value):
        value = jnp.broadcast_to(value, (64, 128))
        return jnp.where(low_half, value[0:32], value[32:64])

    def unpack(value):
        return jnp.concatenate(
            [jnp.where(low_half, value, 0.0), jnp.where(low_half, 0.0, value)], axis=0
        )

    decay2 = jnp.concatenate([decay[...], decay[...]], axis=1)
    weights = [None, decay2]
    for _ in range(7):
        weights.append(weights[-1] * decay2 * math.sqrt(0.5))

    def stack(where, value):
        high, low = split2(value)
        stacked[0:64, where] = high
        stacked[64:128, where] = low

    def coeffs():
        full = lax.dot_general(
            stacked[...], basis2[...], (((1,), (1,)), ((), ())), preferred_element_type=F32
        )
        return pack(full[0:64, 0:128] + full[64:128, 0:128] + full[0:64, 128:256])

    def write_message(slot, coef, scalars):
        high, mid, low = split3(scalars)
        rows = jnp.where(row16 == 0, high, jnp.where(row16 == 1, mid, jnp.where(row16 == 2, low, 0.0)))
        src[slot, 0:32] = coef.astype(BF16)
        src[slot, 32:48] = rows.astype(BF16)

    def read_message(ref):
        return ref[0:32].astype(F32), jnp.sum(ref[32:48].astype(F32), axis=0, keepdims=True)

    def start_sib(step, coef, scalars):
        write_message(3 * step, coef, scalars)
        return send(src.at[3 * step], sib_in.at[step], sib_ss.at[step], sib_rs.at[step], peer(1))

    def start_z(step, copy, coef, scalars):
        copy.wait()
        other, other_scalars = read_message(sib_in.at[step])
        mixed = coef + weights[1] * other
        total, scalars = coef + other, scalars + other_scalars
        write_message(3 * step + 1, total, scalars)
        copies = [
            send(src.at[3 * step + 1], z_in.at[step, k], z_ss.at[step, k], z_rs.at[step, k], peer(m))
            for k, m in enumerate(Z_MASKS)
        ]
        return copies, mixed, total, scalars

    def collect(copies, masks, buffer, mixed, total, scalars):
        for copy in copies:
            copy.wait()
        levels = {}
        for k, mask in enumerate(masks):
            other, other_scalars = read_message(buffer.at[k])
            level = level_of(mask)
            levels[level] = other if level not in levels else levels[level] + other
            scalars = scalars + other_scalars
        for level, other in levels.items():
            mixed = mixed + weights[level] * other
            total = total + other
        return mixed, total, scalars

    def start_xy(step, copies, mixed, total, scalars):
        mixed, total, scalars = collect(copies, Z_MASKS, z_in.at[step], mixed, total, scalars)
        write_message(3 * step + 2, total, scalars)
        copies = [
            send(src.at[3 * step + 2], xy_in.at[step, k], xy_ss.at[step, k], xy_rs.at[step, k], peer(m))
            for k, m in enumerate(XY_MASKS)
        ]
        return copies, mixed, total, scalars

    def finish(step, copies, mixed, total, scalars):
        mixed, _, scalars = collect(copies, XY_MASKS, xy_in.at[step], mixed, total, scalars)
        return mixed, scalars

    def widen(both):
        high, low = split2(both)
        return jnp.concatenate([high, high], axis=1), low

    def far(g, wide, low):
        part = jnp.dot(wide, basis2[:, cols(g)], preferred_element_type=F32)
        return part + jnp.dot(low, basis2[0:128, cols(g)], preferred_element_type=F32)

    def through_gram(wide, low):
        part = jnp.dot(wide, gram[...], preferred_element_type=F32)
        return pack(part + jnp.dot(low, gram[0:128], preferred_element_type=F32))

    high, low = split2(basis[...])
    basis2[0:64] = high
    basis2[64:128] = high
    basis2[128:192] = low
    basis2[192:256] = low
    rr = jnp.zeros((64, 128), F32)
    for g in range(nleaf):
        held = rhs[:, cols(g)]
        put_pool(0, g, held)
        stack(cols(g), held)
        rr = rr + fold(held * held)
    rr_local = lanes(rr)
    coef_r0 = coeffs()
    none = jnp.zeros((1, 128), F32)
    full = lax.dot_general(
        basis2[...], basis2[...], (((1,), (1,)), ((), ())), preferred_element_type=F32
    )
    full = full[0:128, 0:128] + full[0:128, 128:256] + full[128:256, 0:128]
    gram[0:128], gram[128:256] = split2(full)
    row8 = lax.broadcasted_iota(jnp.int32, (8, 128), 0)
    slot = lax.broadcasted_iota(jnp.int32, (8, 128), 1)
    lists[...] = jnp.zeros((8, 128), jnp.int32)
    lists[:, 0:NEAR] = near_list[...]
    row_col = lax.broadcasted_iota(jnp.int32, (8, 8), 0) == lax.broadcasted_iota(jnp.int32, (8, 8), 1)
    lists[:, NEAR : NEAR + 1] = jnp.sum(
        jnp.where(row_col, near_count[...], 0), axis=1, keepdims=True
    )

    center = pts[:, 0:1]
    wide8 = lax.broadcasted_iota(jnp.int32, (8, nleaf * LEAF), 0)

    def parts(coords):
        scaled = (coords - center) * SCALE
        norm = jnp.sum(scaled * scaled, axis=0, keepdims=True)
        return split3(scaled), norm

    def left(coords, first):
        (one, two, three), norm = parts(coords)
        n1, n2, n3 = split3(norm + SCALE * SCALE * 0.0001)
        ends = jnp.where(wide8 < 6, 1.0, 0.0)
        ends = jnp.where(wide8 == 0, n1, jnp.where(wide8 == 1, n2, jnp.where(wide8 == 2, n3, ends)))
        for k, block in enumerate((one, one, two, two, one, three)):
            stage[8 * k : 8 * k + 3, :] = block
        stage[48:56, :] = ends
        for g in range(nleaf):
            left_feat[first + g] = jnp.transpose(stage[:, cols(g)]).astype(BF16)

    def right(coords):
        (one, two, three), norm = parts(coords)
        n1, n2, n3 = split3(norm)
        ends = jnp.where(wide8 < 3, 1.0, 0.0)
        ends = jnp.where(wide8 == 3, n1, jnp.where(wide8 == 4, n2, jnp.where(wide8 == 5, n3, ends)))
        one, two, three = -2.0 * one, -2.0 * two, -2.0 * three
        for k, block in enumerate((one, two, one, two, three, one)):
            stage[8 * k : 8 * k + 3, :] = block
        stage[48:56, :] = ends
        for g in range(nleaf):
            right_feat[g] = stage[:, cols(g)].astype(BF16)

    stage[...] = jnp.zeros(stage.shape, F32)
    right(pts[...])
    left(pts[...], nleaf)

    def tile(leaf, g, one, slope):
        square = jnp.dot(left_feat[leaf], right_feat[g], preferred_element_type=F32)
        root = square * lax.rsqrt(square)
        return (jnp.exp2(-root) * (one + slope * root)).astype(BF16)

    for g in range(nleaf):
        own_tiles[g] = tile(nleaf + g, g, 1.0, LN2)
    pl.semaphore_wait(barrier, len(everyone))

    sib = start_sib(0, coef_r0, none)
    side = both_ways(
        pts, (side_pts.at[0], side_pts.at[1]),
        (side_ss.at[0, 0], side_ss.at[0, 1]), (side_rs.at[0, 0], side_rs.at[0, 1]),
    ) + both_ways(
        lists, (side_lists.at[0], side_lists.at[1]),
        (side_ss.at[1, 0], side_ss.at[1, 1]), (side_rs.at[1, 0], side_rs.at[1, 1]),
    )
    z, mixed, total, scalars = start_z(0, sib, coef_r0, none)
    values = both_ways(
        pool0.at[nleaf : 2 * nleaf], (pool0.at[0:nleaf], pool0.at[2 * nleaf :]),
        (side_ss.at[2, 0], side_ss.at[2, 1]), (side_rs.at[2, 0], side_rs.at[2, 1]),
    )
    for copy in side:
        copy.wait()
    left(side_pts[0], 0)
    left(side_pts[1], 2 * nleaf)

    mine = lists[...]
    counts = mine[:, NEAR : NEAR + 1]
    place = jnp.bitwise_and(jnp.right_shift(mine, 3) - me + 1, ndev - 1)
    index = jnp.clip(place * nleaf + jnp.bitwise_and(mine, nleaf - 1), 0, 3 * nleaf - 1)
    table_v[0] = index
    table_v[2] = (slot < counts).astype(jnp.int32)
    named = jnp.zeros((8, 128), jnp.int32)
    named_active = jnp.zeros((8, 128), jnp.int32)
    for k, theirs in enumerate((side_lists[0], mine, side_lists[1])):
        live = (slot < theirs[:, NEAR : NEAR + 1]).astype(jnp.int32)
        for g in range(nleaf):
            match = theirs == me * nleaf + g
            where = jnp.sum(jnp.where(match, row8 + k * nleaf, 0), axis=0, keepdims=True)
            alive = jnp.sum(jnp.where(match, live, 0), axis=0, keepdims=True)
            named = named + jnp.where(row8 == g, where, 0)
            named_active = named_active + jnp.where(row8 == g, alive, 0)
    table_v[1] = jnp.clip(named, 0, 3 * nleaf - 1)
    table_v[3] = named_active
    times = counts + jnp.sum(jnp.where(slot < NEAR, named_active, 0), axis=1, keepdims=True)
    table_v[4] = jnp.broadcast_to(times, (8, 128))
    to_table = pltpu.make_async_copy(table_v, table, table_sem)
    to_table.start()
    to_table.wait()

    def tile_rows(k):
        return slice(k * LEAF, (k + 1) * LEAF)

    def make_tiles(g):
        for h in range(2):
            for k in range(NEAR):
                one = table[2 + h, g, k].astype(F32)
                tiles[2 * g + h, tile_rows(k), :] = tile(table[h, g, k], g, one, one * LN2)

    def near_leaf(step, g):
        for k in range(NEAR):
            gathered[:, tile_rows(k)] = pool[step][table[0, g, k]]
            gathered[:, tile_rows(NEAR + k)] = pool[step][table[1, g, k]]
        total = jnp.dot(pool[step][nleaf + g], own_tiles[g], preferred_element_type=F32)
        total = table[4, g, 0].astype(F32) * total
        for h in range(2):
            total = total + jnp.dot(
                gathered[:, h * NEAR * LEAF : (h + 1) * NEAR * LEAF], tiles[2 * g + h],
                preferred_element_type=F32,
            )
        near[g] = total
        if step < 2:
            part_src[step][g] = (scale * total).astype(BF16)
        stack(pl.ds(pl.multiple_of(g * LEAF, LEAF), LEAF), total)

    def make_both(g, carry):
        near_leaf(0, g - 1)
        make_tiles(g)
        start_part(0, g - 1)
        return carry

    make_tiles(0)
    for copy in values:
        copy.wait()
    bases = both_ways(
        basis2.at[0:64], (side_basis.at[0], side_basis.at[1]),
        (basis_ss.at[0], basis_ss.at[1]), (basis_rs.at[0], basis_rs.at[1]),
    )
    lax.fori_loop(1, 2, make_both, 0)
    xy, mixed, total, scalars = start_xy(0, z, mixed, total, scalars)
    lax.fori_loop(2, nleaf, make_both, 0)
    near_leaf(0, nleaf - 1)
    start_part(0, nleaf - 1)

    def later_near(step):
        def one_leaf(g, carry):
            near_leaf(step, g)
            if step < 2:
                start_part(step, g)
            return carry

        lax.fori_loop(0, nleaf, one_leaf, 0)

    near_coef = coeffs()
    rb = jnp.zeros((64, 128), F32)
    for g in range(nleaf):
        rb = rb + fold(rhs[:, cols(g)] * near[g])
    near_rb = scale * lanes(rb)
    packed, _ = finish(0, xy, mixed, total, scalars)
    side_coefs = send_coef(0, packed)
    both = unpack(packed)
    wide, low = widen(both)
    coef_b0 = scale * near_coef + through_gram(wide, low)
    scalars = to_row(rr_local, near_rb + lanes(unpack(coef_r0) * both))
    coef = coef_b0
    sib = start_sib(1, coef, scalars)
    for g in range(nleaf):
        value = scale * near[g] + far(g, wide, low)
        b0[:, cols(g)] = value
        put_pool(1, g, value)
    z, mixed, total, scalars = start_z(1, sib, coef, scalars)
    for copy in bases:
        copy.wait()
    side_images(0, side_coefs, lambda leaf, value: value)
    xy, mixed, total, scalars = start_xy(1, z, mixed, total, scalars)
    later_near(1)
    near_coef = coeffs()

    packed, scalars = finish(1, xy, mixed, total, scalars)
    side_coefs = send_coef(1, packed)
    both = unpack(packed)
    wide, low = widen(both)
    rr0, rb0 = from_row(scalars)
    alpha0 = rr0 / (rr0 + rb0)
    coef_y1 = scale * near_coef + through_gram(wide, low)
    coef_r1 = coef_r0 - pack(alpha0) * (coef_r0 + coef_b0)
    coef_b1 = coef_b0 - pack(alpha0) * (coef_b0 + coef_y1)
    rr = jnp.zeros((64, 128), F32)
    rb = jnp.zeros((64, 128), F32)
    for g in range(nleaf):
        one = b0[:, cols(g)]
        held = rhs[:, cols(g)]
        res = held - alpha0 * (held + one)
        r1[:, cols(g)] = res
        nxt = one - alpha0 * (one + scale * near[g])
        b1[:, cols(g)] = nxt
        rr = rr + fold(res * res)
        rb = rb + fold(res * nxt)
    scalars = to_row(lanes(rr), lanes(rb) - alpha0 * lanes(unpack(coef_r1) * both))
    coef = coef_b1
    sib = start_sib(2, coef, scalars)
    for g in range(nleaf):
        part = far(g, wide, low)
        y1[:, cols(g)] = scale * near[g] + part
        nxt = b1[:, cols(g)] - alpha0 * part
        b1[:, cols(g)] = nxt
        put_pool(2, g, nxt)
    z, mixed, total, scalars = start_z(2, sib, coef, scalars)
    side_images(
        1, side_coefs,
        lambda leaf, value: pool1[leaf].astype(F32) * (1.0 - alpha0) - alpha0 * value,
    )
    xy, mixed, total, scalars = start_xy(2, z, mixed, total, scalars)
    later_near(2)

    packed, scalars = finish(2, xy, mixed, total, scalars)
    both = unpack(packed)
    wide, low = widen(both)
    rr1, rb1 = from_row(scalars)
    beta0 = rr1 / rr0
    alpha1 = rr1 / (rr1 + rb1 - beta0 * rr1 / alpha0)
    coef_p1 = coef_r1 + pack(beta0) * coef_r0
    coef_r2 = coef_r1 - pack(alpha1) * (coef_p1 + coef_b1 + pack(beta0) * coef_b0)
    rr = jnp.zeros((64, 128), F32)
    rb = jnp.zeros((64, 128), F32)
    for g in range(nleaf):
        direction = r1[:, cols(g)] + beta0 * rhs[:, cols(g)]
        moved = b1[:, cols(g)] + beta0 * b0[:, cols(g)]
        res = r1[:, cols(g)] - alpha1 * (direction + moved)
        nxt = b1[:, cols(g)] - alpha1 * (moved + scale * near[g] + beta0 * y1[:, cols(g)])
        r2[:, cols(g)] = res
        b2[:, cols(g)] = nxt
        rr = rr + fold(res * res)
        rb = rb + fold(res * nxt)
    scalars = to_row(lanes(rr), lanes(rb) - alpha1 * lanes(unpack(coef_r2) * both))

    last_src[0] = jnp.broadcast_to(scalars, (8, 128))
    copy = send(last_src.at[0], last_sib, sib_ss.at[3], sib_rs.at[3], peer(1))
    copy.wait()
    scalars = scalars + last_sib[0:1]
    for stage_num, (masks, buffer, ss, rs) in enumerate(
        ((Z_MASKS, last_z, z_ss, z_rs), (XY_MASKS, last_xy, xy_ss, xy_rs))
    ):
        last_src[1 + stage_num] = jnp.broadcast_to(scalars, (8, 128))
        copies = [
            send(last_src.at[1 + stage_num], buffer.at[k], ss.at[3, k], rs.at[3, k], peer(m))
            for k, m in enumerate(masks)
        ]
        if stage_num == 0:
            for g in range(nleaf):
                direction = r1[:, cols(g)] + beta0 * rhs[:, cols(g)]
                moved = b1[:, cols(g)] + beta0 * b0[:, cols(g)]
                b2[:, cols(g)] = b2[:, cols(g)] - alpha1 * far(g, wide, low)
                y1[:, cols(g)] = direction
                b0[:, cols(g)] = moved
                r1[:, cols(g)] = alpha0 * rhs[:, cols(g)] + alpha1 * direction
        for copy in copies:
            copy.wait()
        for k in range(len(masks)):
            scalars = scalars + buffer[k, 0:1]
    rr2, rb2 = from_row(scalars)
    beta1 = rr2 / rr1
    alpha2 = rr2 / (rr2 + rb2 - beta1 * rr2 / alpha1)
    for g in range(nleaf):
        direction = r2[:, cols(g)] + beta1 * y1[:, cols(g)]
        moved = b2[:, cols(g)] + beta1 * b0[:, cols(g)]
        r_out[:, cols(g)] = r2[:, cols(g)] - alpha2 * (direction + moved)
        x_out[:, cols(g)] = r1[:, cols(g)] + alpha2 * direction


def body(rhs, points, basis, decay, near_list, near_count):
    nrows, npts = rhs.shape
    nleaf = npts // LEAF
    vmem = pl.BlockSpec(memory_space=pltpu.VMEM)
    field = pltpu.VMEM((nrows, npts), F32)
    dma = pltpu.SemaphoreType.DMA
    shape = jax.ShapeDtypeStruct((nrows, npts), F32)
    return pl.pallas_call(
        kernel,
        out_shape=(shape, shape),
        in_specs=[vmem] * 6,
        out_specs=(vmem, vmem),
        scratch_shapes=[
            pltpu.VMEM((2 * nleaf, NEAR * LEAF, LEAF), BF16),
            pltpu.VMEM((nleaf, LEAF, LEAF), BF16),
            pltpu.VMEM((3 * nleaf, LEAF, 64), BF16),
            pltpu.VMEM((nleaf, 64, LEAF), BF16),
            pltpu.VMEM((64, npts), F32),
            pltpu.VMEM((nrows, 2 * NEAR * LEAF), BF16),
            *[pltpu.VMEM((3 * nleaf, nrows, LEAF), BF16)] * 3,
            pltpu.VMEM((nleaf, nrows, LEAF), F32),
            pltpu.VMEM((256, npts), BF16),
            pltpu.VMEM((128, npts), BF16),
            pltpu.VMEM((256, 128), BF16),
            field, field, field, field, field, field,
            pltpu.VMEM((8, 128), jnp.int32),
            pltpu.VMEM((2, 3, npts), F32),
            pltpu.VMEM((2, 8, 128), jnp.int32),
            pltpu.VMEM((5, 8, 128), jnp.int32),
            pltpu.SMEM((5, 8, 128), jnp.int32),
            *[pltpu.VMEM((nleaf, nrows, LEAF), BF16)] * 2,
            *[pltpu.VMEM((2, nleaf, nrows, LEAF), BF16)] * 2,
            pltpu.VMEM((2, 64, npts), BF16),
            pltpu.VMEM((2, 32, 128), BF16),
            pltpu.VMEM((2, 2, 32, 128), BF16),
            pltpu.VMEM((9, 48, 128), BF16),
            pltpu.VMEM((3, 48, 128), BF16),
            pltpu.VMEM((3, N_Z, 48, 128), BF16),
            pltpu.VMEM((3, N_XY, 48, 128), BF16),
            pltpu.VMEM((3, 8, 128), F32),
            pltpu.VMEM((8, 128), F32),
            pltpu.VMEM((N_Z, 8, 128), F32),
            pltpu.VMEM((N_XY, 8, 128), F32),
            dma((3, 2)), dma((3, 2)), dma((4,)), dma((4,)),
            dma((4, N_Z)), dma((4, N_Z)), dma((4, N_XY)), dma((4, N_XY)),
            dma((2, 2)), dma((2, 2)),
            dma((2,)), dma((2,)), dma((2, 2)), dma((2, 2)),
            dma,
        ],
        compiler_params=pltpu.CompilerParams(
            collective_id=0, has_side_effects=True, vmem_limit_bytes=56 * 2**20
        ),
    )(rhs, points, basis, decay[None, :], near_list, near_count[None, :])


def solution(mesh):
    in_specs = (
        P(None, ("leaf", "sub")),
        P(None, ("leaf", "sub")),
        P(None, ("leaf", "sub")),
        P(),
        P(("leaf", "sub"), None),
        P(("leaf", "sub")),
    )
    out_specs = (P(None, ("leaf", "sub")), P(None, ("leaf", "sub")))
    return jax.shard_map(body, mesh=mesh, in_specs=in_specs, out_specs=out_specs, check_vma=False)
```

time: 86.1 us -> 74.1 us (0.86)
  Pallas kernels: 78.4 us -> 70.6 us
  local copies, waits for them, and re-layouts: 5.93 us -> 2.73 us
    pallas_call x1, Pallas kernels: 78.4 us -> 70.6 us  [body(): pl.pallas_call(kernel, out_shape=(shape, shape), in_specs=[vmem] * 6, out...]
    broadcast_in_dim x2 -> x0, local copies, waits for them, and re-layouts: 1.33 us -> none  [the longest x1 0.73 us: body(): lists = jnp.concatenate([near_list, near_count[:, None]], axis=1)]
    pad x2 -> x0, local copies, waits for them, and re-layouts: 1.23 us -> none  [the longest x1 0.64 us: body(): pts = jnp.pad(points, ((0, 5), (0, 0)))]
    unnamed x8 -> x4, local copies, waits for them, and re-layouts: 3.37 us -> 2.73 us
where the time goes in v2:
time: 74.1 us; the launch traced here: 74 us
  Pallas kernels  70.6 us (95%)
  local copies, waits for them, and re-layouts  2.73 us (4%)
    pallas_call x1, Pallas kernels, body(): pl.pallas_call(kernel, out_shape=(shape, shape), in_specs=[vmem] * 6, out...  70.6 us
    unnamed x4, local copies, waits for them, and re-layouts  2.73 us

profile of v2, /device:TPU:1, one launch (start us, length us, event | category | flops | bytes accessed | tf_op | source)
XLA Modules:
  0.0 74.0 jit_solution(12439756627567558376)
XLA Ops:
  0.6 70.6 %shard_map.77 = (f32[64,2048]{1,0:T(8,128)}, f32[64,2048]{1,0:T(8,128)}) custom-call(f32[64,2048]{1,0:T(8,128)} %rhs.1, f32[3,2048]{1,0:T(4,128)} %pts.1, f32[64,2048]{1,0:T(8,128)} %basis.1, f32[1,64]{1,0:T(1,128)} %bitcast.2, s32[8,8]{1,0:T(8,128)} %near_list.1, s32[1,8]{1,0:T(1,128)} %bitcast.3), custom_call_target="tpu_custom_call" | custom-call | tf_op jit(solution)/shard_map/pallas_call | solution.py:528
  71.2 0.0 copy-start
  71.3 1.9 %copy.10 = f32[64,2048]{1,0:T(8,128)} copy(f32[64,2048]{1,0:T(8,128)} %get-tuple-element.4) | data formatting | bytes 1048576
  73.2 0.0 copy-done
  73.2 0.8 %copy.11 = f32[64,2048]{1,0:T(8,128)} copy(f32[64,2048]{1,0:T(8,128)S(1)} %copy-done) | data formatting | bytes 1048576
Async XLA Ops:
  71.2 1.9 %copy-start = (f32[64,2048]{1,0:T(8,128)S(1)}, f32[64,2048]{1,0:T(8,128)}, u32[]{:S(2)}) copy-start(f32[64,2048]{1,0:T(8,128)} %get-tuple-element.5) | copy-start | bytes 1572868

commit v3 on v2

--- a/solution.py
+++ b/solution.py
@@ -306,7 +306,6 @@
         own_tiles[g] = tile(nleaf + g, g, 1.0, LN2)
     pl.semaphore_wait(barrier, len(everyone))
 
-    sib = start_sib(0, coef_r0, none)
     side = both_ways(
         pts, (side_pts.at[0], side_pts.at[1]),
         (side_ss.at[0, 0], side_ss.at[0, 1]), (side_rs.at[0, 0], side_rs.at[0, 1]),
@@ -314,11 +313,12 @@
         lists, (side_lists.at[0], side_lists.at[1]),
         (side_ss.at[1, 0], side_ss.at[1, 1]), (side_rs.at[1, 0], side_rs.at[1, 1]),
     )
-    z, mixed, total, scalars = start_z(0, sib, coef_r0, none)
     values = both_ways(
         pool0.at[nleaf : 2 * nleaf], (pool0.at[0:nleaf], pool0.at[2 * nleaf :]),
         (side_ss.at[2, 0], side_ss.at[2, 1]), (side_rs.at[2, 0], side_rs.at[2, 1]),
     )
+    sib = start_sib(0, coef_r0, none)
+    z, mixed, total, scalars = start_z(0, sib, coef_r0, none)
     for copy in side:
         copy.wait()
     left(side_pts[0], 0)
@@ -485,7 +485,7 @@
     scalars = to_row(lanes(rr), lanes(rb) - alpha1 * lanes(unpack(coef_r2) * both))
 
     last_src[0] = jnp.broadcast_to(scalars, (8, 128))
-    copy = send(last_src.at[0], last_sib, sib_ss.at[3], sib_rs.at[3], peer(1))
+    copy = send(last_src.at[0, 0:1], last_sib.at[0:1], sib_ss.at[3], sib_rs.at[3], peer(1))
     copy.wait()
     scalars = scalars + last_sib[0:1]
     for stage_num, (masks, buffer, ss, rs) in enumerate(
@@ -493,7 +493,7 @@
     ):
         last_src[1 + stage_num] = jnp.broadcast_to(scalars, (8, 128))
         copies = [
-            send(last_src.at[1 + stage_num], buffer.at[k], ss.at[3, k], rs.at[3, k], peer(m))
+            send(last_src.at[1 + stage_num, 0:1], buffer.at[k, 0:1], ss.at[3, k], rs.at[3, k], peer(m))
             for k, m in enumerate(masks)
         ]
         if stage_num == 0:
@@ -518,6 +518,15 @@
         x_out[:, cols(g)] = r1[:, cols(g)] + alpha2 * direction
 
 
+def place(x_in, r_in, x_out, r_out, sems):
+    first = pltpu.make_async_copy(x_in, x_out, sems.at[0])
+    second = pltpu.make_async_copy(r_in, r_out, sems.at[1])
+    first.start()
+    second.start()
+    first.wait()
+    second.wait()
+
+
 def body(rhs, points, basis, decay, near_list, near_count):
     nrows, npts = rhs.shape
     nleaf = npts // LEAF
@@ -525,7 +534,7 @@
     field = pltpu.VMEM((nrows, npts), F32)
     dma = pltpu.SemaphoreType.DMA
     shape = jax.ShapeDtypeStruct((nrows, npts), F32)
-    return pl.pallas_call(
+    outs = pl.pallas_call(
         kernel,
         out_shape=(shape, shape),
         in_specs=[vmem] * 6,
@@ -571,6 +580,14 @@
             collective_id=0, has_side_effects=True, vmem_limit_bytes=56 * 2**20
         ),
     )(rhs, points, basis, decay[None, :], near_list, near_count[None, :])
+    anywhere = pl.BlockSpec(memory_space=pl.ANY)
+    return pl.pallas_call(
+        place,
+        out_shape=(shape, shape),
+        in_specs=[anywhere] * 2,
+        out_specs=(anywhere, anywhere),
+        scratch_shapes=[dma((2,))],
+    )(*outs)
 
 
 def solution(mesh):

time: 74.1 us -> 104 us (1.40)
  Pallas kernels: 70.6 us -> 103 us
  local copies, waits for them, and re-layouts: 2.73 us -> 0 us
    pallas_call x0 -> x1, Pallas kernels: none -> 32.9 us  [body(): pl.pallas_call(place, out_shape=(shape, shape), in_specs=[anywhere] * 2,...]
    unnamed x4 -> x0, local copies, waits for them, and re-layouts: 2.73 us -> none
where the time goes in v3:
time: 104 us
  Pallas kernels  103 us (99%)
    pallas_call x1, Pallas kernels, body(): pl.pallas_call(kernel, out_shape=(shape, shape), in_specs=[vmem] * 6, out...  70.3 us
    pallas_call x1, Pallas kernels, body(): pl.pallas_call(place, out_shape=(shape, shape), in_specs=[anywhere] * 2,...  32.9 us

profile of v3, /device:TPU:1, one launch (start us, length us, event | category | flops | bytes accessed | tf_op | source)
XLA Modules:
  0.0 103.9 jit_solution(14649360195925510846)
XLA Ops:
  0.6 70.3 %shard_map.77 = (f32[64,2048]{1,0:T(8,128)}, f32[64,2048]{1,0:T(8,128)}) custom-call(f32[64,2048]{1,0:T(8,128)} %rhs.1, f32[3,2048]{1,0:T(4,128)} %pts.1, f32[64,2048]{1,0:T(8,128)} %basis.1, f32[1,64]{1,0:T(1,128)} %bitcast.2, s32[8,8]{1,0:T(8,128)} %near_list.1, s32[1,8]{1,0:T(1,128)} %bitcast.3), custom_call_target="tpu_custom_call" | custom-call | tf_op jit(solution)/shard_map/pallas_call | solution.py:537
  70.9 32.9 %shard_map.78 = (f32[64,2048]{1,0:T(8,128)}, f32[64,2048]{1,0:T(8,128)}) custom-call(f32[64,2048]{1,0:T(8,128)} %get-tuple-element.4.x_in, f32[64,2048]{1,0:T(8,128)} %get-tuple-element.5.r_in), custom_call_target="tpu_custom_call" | custom-call | tf_op jit(solution)/shard_map/pallas_call | solution.py:584

commit v4 on v3

--- a/solution.py
+++ b/solution.py
@@ -518,13 +518,22 @@
         x_out[:, cols(g)] = r1[:, cols(g)] + alpha2 * direction
 
 
-def place(x_in, r_in, x_out, r_out, sems):
-    first = pltpu.make_async_copy(x_in, x_out, sems.at[0])
-    second = pltpu.make_async_copy(r_in, r_out, sems.at[1])
-    first.start()
-    second.start()
-    first.wait()
-    second.wait()
+def place(x_in, r_in, x_out, r_out, hold, sems):
+    reads = [
+        pltpu.make_async_copy(source, hold.at[k], sems.at[k])
+        for k, source in enumerate((x_in, r_in))
+    ]
+    for copy in reads:
+        copy.start()
+    writes = [
+        pltpu.make_async_copy(hold.at[k], target, sems.at[2 + k])
+        for k, target in enumerate((x_out, r_out))
+    ]
+    for read, write in zip(reads, writes):
+        read.wait()
+        write.start()
+    for copy in writes:
+        copy.wait()
 
 
 def body(rhs, points, basis, decay, near_list, near_count):
@@ -586,7 +595,7 @@
         out_shape=(shape, shape),
         in_specs=[anywhere] * 2,
         out_specs=(anywhere, anywhere),
-        scratch_shapes=[dma((2,))],
+        scratch_shapes=[pltpu.VMEM((2, nrows, npts), F32), dma((4,))],
     )(*outs)
 
 

time: 104 us -> 73.2 us (0.70)
  Pallas kernels: 103 us -> 72.3 us
    pallas_call x1, Pallas kernels: 32.9 us -> 2.04 us  [body(): pl.pallas_call(place, out_shape=(shape, shape), in_specs=[anywhere] * 2,...]
where the time goes in v4:
time: 73.2 us; the launch traced here: 73.1 us
  Pallas kernels  72.3 us (99%)
  between operations  0.8 us (1%)
    pallas_call x1, Pallas kernels, body(): pl.pallas_call(kernel, out_shape=(shape, shape), in_specs=[vmem] * 6, out...  70.3 us
    pallas_call x1, Pallas kernels, body(): pl.pallas_call(place, out_shape=(shape, shape), in_specs=[anywhere] * 2,...  2.04 us

profile of v4, /device:TPU:1, one launch (start us, length us, event | category | flops | bytes accessed | tf_op | source)
XLA Modules:
  0.0 73.1 jit_solution(2327085812445112486)
XLA Ops:
  0.6 70.3 %shard_map.77 = (f32[64,2048]{1,0:T(8,128)}, f32[64,2048]{1,0:T(8,128)}) custom-call(f32[64,2048]{1,0:T(8,128)} %rhs.1, f32[3,2048]{1,0:T(4,128)} %pts.1, f32[64,2048]{1,0:T(8,128)} %basis.1, f32[1,64]{1,0:T(1,128)} %bitcast.2, s32[8,8]{1,0:T(8,128)} %near_list.1, s32[1,8]{1,0:T(1,128)} %bitcast.3), custom_call_target="tpu_custom_call" | custom-call | tf_op jit(solution)/shard_map/pallas_call | solution.py:546
  70.9 2.0 %shard_map.78 = (f32[64,2048]{1,0:T(8,128)}, f32[64,2048]{1,0:T(8,128)}) custom-call(f32[64,2048]{1,0:T(8,128)} %get-tuple-element.4.x_in, f32[64,2048]{1,0:T(8,128)} %get-tuple-element.5.r_in), custom_call_target="tpu_custom_call" | custom-call | tf_op jit(solution)/shard_map/pallas_call | solution.py:593
